TPU v7x, 32 devices: a whole 2x2x4 slice. The times are simulated.
32 devices in a mesh: sub: 8 (over y, x, core), col: 4 (over z).
Axes of the slice: x: 2, y: 2, z: 4, core: 2. Of those that a mesh axis runs over, the one named last changes fastest.
Arguments:
- perm: float32 [512, 512, 128], P('sub', 'col'), may hold values from 0.1 to 10
- accum: float32 [512, 512, 128], P('sub', 'col'), may hold values from 0.05 to 2
- rhs: float32 [512, 512, 128], P('sub', 'col'), may hold values from -24 to 24
- depth_x: int32 [16, 512], P('sub', 'col'), may hold values from 0 to 4, as said below
- depth_y: int32 [512, 8], P('sub', 'col'), may hold values from 0 to 4, as said below
Outputs:
- pressure: float32 [512, 512, 128], P('sub', 'col')
Inputs may be any that keep to these rules, and one draw needn't show every extreme that they name: Both sides of one interface share its depth: depth_x[2 s + 1, j] = depth_x[2 s + 2, j] and depth_y[i, 2 c + 1] = depth_y[i, 2 c + 2]; faces on the grid's boundary have depth 0; the depth 4 occurs. `depth_y`: as for depth_x, along the second dimension.
All inputs are finite; a program needn't handle non-finite values.
Results may differ from a plain program's by a relative error of at most 0.0003.
Values sent between devices are 32-bit elements; how exact they have to be, the bound alone decides.
A program may use at most 192 MiB of HBM per device.

v0:
```python
import functools

import jax
import jax.numpy as jnp
from jax import lax
from jax.experimental import pallas as pl
from jax.experimental.pallas import tpu as pltpu
from jax.sharding import PartitionSpec as P

OVL = 4
VERTICAL = 0.1
MESH = pl.DeviceIdType.MESH

PADX = 5
PADY = 8
DIRS = ((-1, 0), (1, 0), (0, -1), (0, 1), (-1, -1), (-1, 1), (1, -1), (1, 1))


def recip(value):
    return pl.reciprocal(value, approx=True)


def harmonic(first, second):
    return 2.0 * first * second * recip(first + second)


def kernel(n_sub, n_col, bx, by, perm, accum, rhs, depth_x, depth_y, out,
           dx_ref, dy_ref, lane_y, pm, w, r, b, c, fx, fy, fz, pr, sx, sy, ssem, rsem, lsem):
    nz = 128
    s = lax.axis_index("sub")
    k = lax.axis_index("col")
    ex, ey = bx + 2 * PADX, by + 2 * PADY
    nbx, nby = (bx + 8) // 8, (by + 8) // 8
    x_end, y_end = PADX + bx, PADY + by

    def exists(d):
        ok = None
        for coord, step, count in ((s, d[0], n_sub), (k, d[1], n_col)):
            if step == -1:
                test = coord > 0
            elif step == 1:
                test = coord < count - 1
            else:
                continue
            ok = test if ok is None else ok & test
        return ok

    def device(d):
        return (s + d[0], k + d[1])

    own_x, own_y = pl.ds(PADX, bx), pl.ds(PADY, by)
    local = [
        pltpu.make_async_copy(src, dst.at[own_x, own_y, :], lsem.at[i])
        for i, (src, dst) in enumerate(((perm, pm), (accum, w), (rhs, r)))
    ]
    for copy in local:
        copy.start()

    def fill(ref, value):
        ref[0:PADX, :, :] = jnp.full((PADX, ey, nz), value, jnp.float32)
        ref[x_end:ex, :, :] = jnp.full((PADX, ey, nz), value, jnp.float32)
        ref[PADX:x_end, 0:PADY, :] = jnp.full((bx, PADY, nz), value, jnp.float32)
        ref[PADX:x_end, y_end:ey, :] = jnp.full((bx, PADY, nz), value, jnp.float32)

    fill(pm, 1.0)
    fill(w, 1.0)
    fill(r, 0.0)
    fill(b, 0.0)
    fill(c, 0.0)
    fill(pr, 0.0)
    sx[...] = jnp.zeros(sx.shape, jnp.float32)
    sy[...] = jnp.zeros(sy.shape, jnp.float32)

    dx_ref[...] = jnp.zeros(dx_ref.shape, jnp.int32)
    dy_ref[...] = jnp.zeros(dy_ref.shape, jnp.int32)
    for side in range(2):
        dx_ref[side, own_y, :] = jnp.broadcast_to(depth_x[side:side + 1, :], (nz, by)).T
        lane_y[side] = jnp.broadcast_to(depth_y[:, side:side + 1], (bx, nz))

    def spread_depth(i, carry):
        for side in range(2):
            dy_ref[side, PADX + i] = jnp.broadcast_to(lane_y[side, pl.ds(i, 1), :], (8, nz))
        return carry

    barrier = pltpu.get_barrier_semaphore()
    arrivals = jnp.int32(0)
    for d in DIRS:
        @pl.when(exists(d))
        def _(d=d):
            pl.semaphore_signal(barrier, inc=1, device_id=device(d), device_id_type=MESH)
        arrivals = arrivals + jnp.where(exists(d), 1, 0).astype(jnp.int32)
    pl.semaphore_wait(barrier, arrivals)

    counter = [0]

    def remote(src, dst, d):
        i = counter[0]
        counter[0] += 1
        return d, pltpu.make_async_remote_copy(
            src_ref=src, dst_ref=dst, send_sem=ssem.at[i], recv_sem=rsem.at[i],
            device_id=device(d), device_id_type=MESH)

    def start(copies):
        for d, copy in copies:
            pl.when(exists(d))(copy.start)

    def wait_recv(copies):
        for d, copy in copies:
            pl.when(exists((-d[0], -d[1])))(copy.wait_recv)

    def wait_send(copies):
        for d, copy in copies:
            pl.when(exists(d))(copy.wait_send)

    def halo(src, ox, oy, dst, d, width):
        def span(step, offset, extent, pad, thick):
            if step == 0:
                return pl.ds(offset, extent), pl.ds(pad, extent)
            if step == 1:
                return pl.ds(offset + extent - thick, thick), pl.ds(pad - thick, thick)
            return pl.ds(offset, thick), pl.ds(pad + extent, thick)

        sxs, dxs = span(d[0], ox, bx, PADX, width)
        sys_, dys = span(d[1], oy, by, PADY, width)
        return remote(src.at[sxs, sys_, :], dst.at[dxs, dys, :], d)

    halos = [halo(perm, 0, 0, pm, d, 5) for d in DIRS]
    halos += [halo(accum, 0, 0, w, d, 4) for d in DIRS[:4]]
    halos += [halo(rhs, 0, 0, r, d, 4) for d in DIRS[:4]]
    start(halos)
    lax.fori_loop(0, bx, spread_depth, 0, unroll=8)

    def at(ref, x0, y0, rows=8, columns=8):
        return ref[pl.ds(x0, rows), pl.ds(y0, columns), :]

    def stencil(ref, x0, y0):
        wide = at(ref, x0 - 1, y0, 10)
        centre = wide[1:9]
        face = at(fx, x0 - 1, y0, 9)
        total = face[0:8] * wide[0:8] + face[1:9] * wide[2:10]
        total = total + at(fy, x0, y0) * at(ref, x0, y0 - 1)
        total = total + at(fy, x0, y0 + 1) * at(ref, x0, y0 + 1)
        up = at(fz, x0, y0)
        total = total + up * pltpu.roll(centre, nz - 1, 2)
        total = total + pltpu.roll(up * centre, 1, 2)
        return total, centre

    def coefficients(x0, y0, frame):
        wide = at(pm, x0 - 1, y0, 10)
        centre = wide[1:9]
        across_x = harmonic(wide[0:9], wide[1:10])
        across_y0 = harmonic(at(pm, x0, y0 - 1), centre)
        across_y1 = harmonic(centre, at(pm, x0, y0 + 1))
        lane = lax.broadcasted_iota(jnp.int32, (8, 8, nz), 2)
        up = VERTICAL * harmonic(centre, pltpu.roll(centre, nz - 1, 2))
        up = jnp.where(lane < nz - 1, up, 0.0)
        if frame:
            row = x0 - 1 + lax.broadcasted_iota(jnp.int32, (9, 8, nz), 0)
            shut = (row == jnp.where(s == 0, PADX - 1, -1)) | (
                row == jnp.where(s == n_sub - 1, x_end - 1, -1))
            across_x = jnp.where(shut, 0.0, across_x)
            column = y0 + lax.broadcasted_iota(jnp.int32, (8, 8, nz), 1)
            first = jnp.where(k == 0, PADY, -1)
            last = jnp.where(k == n_col - 1, y_end, -1)
            across_y0 = jnp.where((column == first) | (column == last), 0.0, across_y0)
            across_y1 = jnp.where((column + 1 == first) | (column + 1 == last), 0.0, across_y1)
        faces = (across_x[0:8] + across_x[1:9] + across_y0 + across_y1
                 + up + pltpu.roll(up, 1, 2))
        if frame:
            row = row[0:8] + 1
            low_x, high_x = dx_ref[0, pl.ds(y0, 8), :], dx_ref[1, pl.ds(y0, 8), :]
            low_y, high_y = dy_ref[0, pl.ds(x0, 8), :, :], dy_ref[1, pl.ds(x0, 8), :, :]
            member = (row >= PADX) & (row < x_end) & (column >= PADY) & (column < y_end)
            member = member | ((row < PADX) & (PADX - 1 - row < low_x[None]))
            member = member | ((row >= x_end) & (row - x_end < high_x[None]))
            member = member | ((column < PADY) & (PADY - 1 - column < low_y))
            member = member | ((column >= y_end) & (column - y_end < high_y))
            c[pl.ds(x0, 8), pl.ds(y0, 8), :] = jnp.where(member, faces, -1.0)
        fx[pl.ds(x0 - 1, 9), pl.ds(y0, 8), :] = across_x
        fy[pl.ds(x0, 8), pl.ds(y0, 8), :] = across_y0
        fy[pl.ds(x0, 8), pl.ds(y0 + 1, 8), :] = across_y1
        fz[pl.ds(x0, 8), pl.ds(y0, 8), :] = up
        if not frame:
            inverse = recip(at(w, x0, y0) + faces)
            w[pl.ds(x0, 8), pl.ds(y0, 8), :] = inverse
            b[pl.ds(x0, 8), pl.ds(y0, 8), :] = inverse * at(r, x0, y0)

    def weights(x0, y0):
        faces = at(c, x0, y0)
        inverse = jnp.where(faces >= 0.0, recip(at(w, x0, y0) + jnp.maximum(faces, 0.0)), 0.0)
        w[pl.ds(x0, 8), pl.ds(y0, 8), :] = inverse
        b[pl.ds(x0, 8), pl.ds(y0, 8), :] = inverse * at(r, x0, y0)

    def second_sweep(x0, y0):
        total, _ = stencil(b, x0, y0)
        c[pl.ds(x0, 8), pl.ds(y0, 8), :] = at(b, x0, y0) + at(w, x0, y0) * total

    def third_sweep(x0, y0):
        total, _ = stencil(c, x0, y0)
        return at(b, x0, y0) + at(w, x0, y0) * total

    def third_frame(x0, y0):
        b[pl.ds(x0, 8), pl.ds(y0, 8), :] = third_sweep(x0, y0)

    def third_first(x0, y0):
        pr[pl.ds(x0, 8), pl.ds(y0, 8), :] = third_sweep(x0, y0)

    def third_last(x0, y0):
        pr[pl.ds(x0, 8), pl.ds(y0, 8), :] = at(pr, x0, y0) + third_sweep(x0, y0)

    def restart(x0, y0):
        total, centre = stencil(pr, x0, y0)
        weight = at(w, x0, y0)
        b[pl.ds(x0, 8), pl.ds(y0, 8), :] = jnp.where(
            weight > 0.0, weight * (at(r, x0, y0) + total) - centre, 0.0)

    def loop(low, high, body, unroll):
        full = (high - low) // unroll

        def several(i, carry):
            for u in range(unroll):
                body(low + i * unroll + u)
            return carry
        lax.fori_loop(0, full, several, 0)
        for i in range(low + full * unroll, high):
            body(i)

    def region(body, x_low, x_high, y_low, y_high):
        def column(j):
            for i in range(x_low, x_high):
                body(1 + 8 * i, 4 + 8 * j)
        loop(y_low, y_high, column, 2)

    def ring(body, depth, unroll, between=lambda: None):
        low_y, high_y = depth, nby - 1 - depth
        low_x, high_x = depth, nbx - 1 - depth

        def along_y(j):
            body(1 + 8 * low_x, 4 + 8 * j)
            body(1 + 8 * high_x, 4 + 8 * j)
        loop(low_y, high_y + 1, along_y, unroll)
        between()

        def along_x(i):
            body(1 + 8 * i, 4 + 8 * low_y)
            body(1 + 8 * i, 4 + 8 * high_y)
        loop(low_x + 1, high_x, along_x, unroll)

    def interior(body):
        region(body, 1, nbx - 1, 1, nby - 1)

    def inner(body):
        region(body, 2, nbx - 2, 2, nby - 2)

    def frame(body, unroll=4, between=lambda: None):
        ring(body, 0, unroll, between)

    def border(body):
        ring(body, 1, 4)

    def gather(turn, x0, y0, side_x, side_y):
        own = at(b, x0, y0, 4)
        before = at(pr, x0, y0, 4)
        row = x0 + lax.broadcasted_iota(jnp.int32, (4, 8, nz), 0)
        column = y0 + lax.broadcasted_iota(jnp.int32, (4, 8, nz), 1)
        total = own
        if side_x is not None:
            total = total + sx[turn, side_x, :, pl.ds(y0 - PADY, 8), :]
        if side_y is not None:
            total = total + sy[turn, side_y, pl.ds(x0 - PADX, 4), :, :]
        cover = 1.0 + (row - PADX < dx_ref[0, pl.ds(y0, 8), :][None]).astype(jnp.float32)
        cover = cover + (x_end - 1 - row < dx_ref[1, pl.ds(y0, 8), :][None]).astype(jnp.float32)
        cover = cover + (column - PADY < dy_ref[0, pl.ds(x0, 4), :, :]).astype(jnp.float32)
        cover = cover + (y_end - 1 - column < dy_ref[1, pl.ds(x0, 4), :, :]).astype(jnp.float32)
        total = total / cover
        if turn == 1:
            total = before + total
        if side_x is None:
            edge = (column < PADY + 4) if side_y == 0 else (column >= y_end - 4)
            total = jnp.where(edge, total, before)
        pr[pl.ds(x0, 4), pl.ds(y0, 8), :] = total

    def gather_all(turn):
        top = x_end - 4
        for side_y, y0 in ((0, PADY), (1, y_end - 8)):
            gather(turn, PADX, y0, 0, side_y)
            gather(turn, top, y0, 1, side_y)

            def along_x(i, carry, y0=y0, side_y=side_y):
                gather(turn, PADX + 4 * i, y0, None, side_y)
                return carry
            lax.fori_loop(1, bx // 4 - 1, along_x, 0)

        def along_y(j, carry):
            gather(turn, PADX, PADY + 8 * j, 0, None)
            gather(turn, top, PADY + 8 * j, 1, None)
            return carry
        lax.fori_loop(1, by // 8 - 1, along_y, 0)

    def returns(turn):
        return [
            remote(b.at[pl.ds(PADX - 4, 4), own_y, :], sx.at[turn, 1], (-1, 0)),
            remote(b.at[pl.ds(x_end, 4), own_y, :], sx.at[turn, 0], (1, 0)),
            remote(b.at[own_x, pl.ds(4, 4), :], sy.at[turn, 1, :, 4:8, :], (0, -1)),
            remote(b.at[own_x, pl.ds(y_end, 4), :], sy.at[turn, 0, :, 0:4, :], (0, 1)),
        ]

    for copy in local:
        copy.wait()
    interior(functools.partial(coefficients, frame=False))
    wait_recv(halos[:8])
    frame(functools.partial(coefficients, frame=True), 1)
    inner(second_sweep)
    wait_recv(halos[8:])
    frame(weights)
    frame(second_sweep)
    border(second_sweep)
    back = returns(0)
    frame(third_frame, 4, lambda: start(back[:2]))
    start(back[2:])
    interior(third_first)
    wait_recv(back)
    gather_all(0)
    spread = [halo(pr, PADX, PADY, pr, d, 5) for d in DIRS]
    start(spread)
    interior(restart)
    inner(second_sweep)
    wait_send(back)
    wait_recv(spread)
    frame(restart)
    frame(second_sweep)
    border(second_sweep)
    back = returns(1)
    frame(third_frame, 4, lambda: start(back[:2]))
    start(back[2:])
    wait_send(spread)
    interior(third_last)

    def store(i, x0, rows, y0, columns):
        return pltpu.make_async_copy(
            pr.at[pl.ds(PADX + x0, rows), pl.ds(PADY + y0, columns), :],
            out.at[pl.ds(x0, rows), pl.ds(y0, columns), :], lsem.at[i])

    middle = store(0, 4, bx - 8, 8, by - 16)
    edges = [store(1, 0, 4, 0, by), store(2, bx - 4, 4, 0, by),
             store(3, 4, bx - 8, 0, 8), store(4, 4, bx - 8, by - 8, 8)]
    middle.start()
    wait_recv(back)
    gather_all(1)
    for copy in edges:
        copy.start()
    wait_send(halos)
    wait_send(back)
    for copy in (*edges, middle):
        copy.wait()


def relay(source, target, held, sem):
    rows = source.shape[0] // 8
    spans = [pl.ds(i * rows, rows) for i in range(8)]
    reads = [pltpu.make_async_copy(source.at[span], held.at[span], sem.at[0, i])
             for i, span in enumerate(spans)]
    writes = [pltpu.make_async_copy(held.at[span], target.at[span], sem.at[1, i])
              for i, span in enumerate(spans)]
    for copy in reads:
        copy.start()
    for read, write in zip(reads, writes):
        read.wait()
        write.start()
    for copy in writes:
        copy.wait()


def shards(n_sub, n_col, perm, accum, rhs, depth_x, depth_y):
    bx, by, nz = perm.shape
    ex, ey = bx + 2 * PADX, by + 2 * PADY
    field = pltpu.VMEM((ex, ey, nz), jnp.float32)
    hbm = pl.BlockSpec(memory_space=pl.ANY)
    vmem = pl.BlockSpec(memory_space=pltpu.VMEM)
    copies = 16 + 4 + 8 + 4
    result = pl.pallas_call(
        functools.partial(kernel, n_sub, n_col, bx, by),
        out_shape=jax.ShapeDtypeStruct((bx, by, nz), jnp.float32),
        in_specs=[hbm, hbm, hbm, vmem, vmem],
        out_specs=hbm,
        scratch_shapes=[
            pltpu.VMEM((2, ey, nz), jnp.int32),
            pltpu.VMEM((2, ex, 8, nz), jnp.int32),
            pltpu.VMEM((2, bx, nz), jnp.int32),
        ] + [field] * 9 + [
            pltpu.VMEM((2, 2, 4, by, nz), jnp.float32),
            pltpu.VMEM((2, 2, bx, 8, nz), jnp.float32),
            pltpu.SemaphoreType.DMA((copies,)),
            pltpu.SemaphoreType.DMA((copies,)),
            pltpu.SemaphoreType.DMA((5,)),
        ],
        compiler_params=pltpu.CompilerParams(
            collective_id=0, has_side_effects=True, vmem_limit_bytes=60 * 1024 * 1024),
        cost_estimate=pl.CostEstimate(
            flops=120 * bx * by * nz, bytes_accessed=16 * bx * by * nz, transcendentals=0),
    )(perm, accum, rhs, depth_x, depth_y)
    return pl.pallas_call(
        relay,
        out_shape=jax.ShapeDtypeStruct((bx, by, nz), jnp.float32),
        in_specs=[hbm], out_specs=hbm,
        scratch_shapes=[pltpu.VMEM((bx, by, nz), jnp.float32), pltpu.SemaphoreType.DMA((2, 8))],
        compiler_params=pltpu.CompilerParams(vmem_limit_bytes=16 * 1024 * 1024),
    )(result)


def solution(mesh):
    placed = (
        P("sub", "col", None),
        P("sub", "col", None),
        P("sub", "col", None),
        P("sub", "col"),
        P("sub", "col"),
    )
    return jax.shard_map(
        functools.partial(shards, mesh.shape["sub"], mesh.shape["col"]),
        mesh=mesh, in_specs=placed, out_specs=P("sub", "col", None), check_vma=False
    )
```

profile of v0, /device:TPU:19, one launch (start us, length us, event | category | flops | bytes accessed | tf_op | source)
XLA Modules:
  0.0 63.5 jit_solution(15857846020128224135)
XLA Ops:
  0.0 1.4 %copy.6.depth_y = s32[64,2]{1,0:T(8,128)} copy(s32[64,2]{0,1:T(2,128)} %param.9) | data formatting | bytes 1024 | tf_op args[4]
  1.4 57.5 %shard_map.55.source = f32[64,128,128]{2,1,0:T(8,128)} custom-call(f32[64,128,128]{2,1,0:T(8,128)} %perm.1, f32[64,128,128]{2,1,0:T(8,128)} %accum.1, f32[64,128,128]{2,1,0:T(8,128)} %rhs.1, s32[2,128]{1,0:T(2,128)} %depth_x.1, s32[64,2]{1,0:T(8,128)} %copy.6.depth_y), custom_call_target="tpu_custom_call" | custom-call | flops 125829120 | bytes 16777216 | tf_op jit(solution)/shard_map/pallas_call | solution.py:381
  58.9 0.0 copy-start
  58.9 2.2 %copy-done = f32[64,128,128]{2,1,0:T(8,128)S(1)} copy-done((f32[64,128,128]{2,1,0:T(8,128)S(1)}, f32[64,128,128]{2,1,0:T(8,128)}, u32[]{:S(2)}) %copy-start) | copy-done | bytes 4194328
  61.1 2.4 %shard_map.56 = f32[64,128,128]{2,1,0:T(8,128)} custom-call(f32[64,128,128]{2,1,0:T(8,128)S(1)} %copy-done), custom_call_target="tpu_custom_call" | custom-call | tf_op jit(solution)/shard_map/pallas_call | solution.py:402
Async XLA Ops:
  58.9 2.2 %copy-start = (f32[64,128,128]{2,1,0:T(8,128)S(1)}, f32[64,128,128]{2,1,0:T(8,128)}, u32[]{:S(2)}) copy-start(f32[64,128,128]{2,1,0:T(8,128)} %shard_map.55.source) | copy-start | bytes 12582916
where the time goes:
time: 63.7 us; the launch traced here: 63.5 us
  Pallas kernels  59.9 us (94%)
  local copies, waits for them, and re-layouts  3.56 us (6%)
    pallas_call x1, Pallas kernels, shards(): pl.pallas_call(functools.partial(kernel, n_sub, n_col, bx, by), out_shape...  57.5 us
    unnamed x3, local copies, waits for them, and re-layouts  3.56 us
    pallas_call x1, Pallas kernels, shards(): pl.pallas_call(relay, out_shape=jax.ShapeDtypeStruct((bx, by, nz), jnp.fl...  2.42 us

commit v1 on v0

v1 whole, which is shorter than its diff:
```python
import functools

import jax
import jax.numpy as jnp
from jax import lax
from jax.experimental import pallas as pl
from jax.experimental.pallas import tpu as pltpu
from jax.sharding import PartitionSpec as P

OVL = 4
VERTICAL = 0.1
MESH = pl.DeviceIdType.MESH

PADX = 3
PADY = 8
DIRS = ((-1, 0), (1, 0), (0, -1), (0, 1), (-1, -1), (-1, 1), (1, -1), (1, 1))
CHUNK = 8


def recip(value):
    return pl.reciprocal(value, approx=True)


def harmonic(first, second):
    return first * second * recip(first + second)


def kernel(n_sub, n_col, bx, by, perm, accum, rhs, depth_x, depth_y, out,
           dx_ref, dy_ref, hx, hy, pm, w, r, b, fx, fy, fz, pr,
           xw, xb, xc, yw, yb, yc, ssem, rsem, lsem):
    nz = 128
    s = lax.axis_index("sub")
    k = lax.axis_index("col")
    ex, ey = bx + 2 * PADX, by + 2 * PADY
    c = pm
    n_a, n_q = bx // 8 - 1, by // 8 + 1
    x_end, y_end = PADX + bx, PADY + by

    def exists(d):
        ok = None
        for coord, step, count in ((s, d[0], n_sub), (k, d[1], n_col)):
            if step == -1:
                test = coord > 0
            elif step == 1:
                test = coord < count - 1
            else:
                continue
            ok = test if ok is None else ok & test
        return ok

    def device(d):
        return (s + d[0], k + d[1])

    own_x, own_y = pl.ds(PADX, bx), pl.ds(PADY, by)

    def local(n):
        here = pl.ds(n * CHUNK, CHUNK)
        there = pl.ds(PADX + n * CHUNK, CHUNK)
        return [pltpu.make_async_copy(src.at[here], dst.at[there, own_y, :], lsem.at[i, n])
                for i, (src, dst) in enumerate(((perm, pm), (accum, w), (rhs, r)))]

    for n in range(bx // CHUNK):
        for copy in local(n):
            copy.start()

    def each(count, body):
        def step(i, carry):
            body(i)
            return carry
        lax.fori_loop(0, count, step, 0)

    def fill(value, *refs):
        for ref in refs:
            for x0 in (0, x_end):
                ref[x0:x0 + PADX, :, :] = jnp.full((PADX, ey, nz), value, jnp.float32)

        def rows(i):
            for ref in refs:
                for y0 in (0, y_end):
                    ref[pl.ds(PADX + 8 * i, 8), y0:y0 + PADY, :] = jnp.full((8, PADY, nz), value, jnp.float32)
        each(bx // 8, rows)

    fill(1.0, pm, w)
    fill(0.0, r, pr)
    hx[...] = jnp.zeros(hx.shape, jnp.int32)
    hy[...] = jnp.zeros(hy.shape, jnp.int32)

    barrier = pltpu.get_barrier_semaphore()
    arrivals = jnp.int32(0)
    for d in DIRS:
        @pl.when(exists(d))
        def _(d=d):
            pl.semaphore_signal(barrier, inc=1, device_id=device(d), device_id_type=MESH)
        arrivals = arrivals + jnp.where(exists(d), 1, 0).astype(jnp.int32)
    pl.semaphore_wait(barrier, arrivals)

    counter = [0]

    def remote(src, dst, d):
        i = counter[0]
        counter[0] += 1
        return d, pltpu.make_async_remote_copy(
            src_ref=src, dst_ref=dst, send_sem=ssem.at[i], recv_sem=rsem.at[i],
            device_id=device(d), device_id_type=MESH)

    def start(copies):
        for d, copy in copies:
            pl.when(exists(d))(copy.start)

    def wait_recv(copies):
        for d, copy in copies:
            pl.when(exists((-d[0], -d[1])))(copy.wait_recv)

    def wait_send(copies):
        for d, copy in copies:
            pl.when(exists(d))(copy.wait_send)

    def halo(src, ox, oy, dst, d, width):
        def span(step, offset, extent, pad, thick):
            if step == 0:
                return pl.ds(offset, extent), pl.ds(pad, extent)
            if step == 1:
                return pl.ds(offset + extent - thick, thick), pl.ds(pad - thick, thick)
            return pl.ds(offset, thick), pl.ds(pad + extent, thick)

        sxs, dxs = span(d[0], ox, bx, PADX, width)
        sys_, dys = span(d[1], oy, by, PADY, width)
        return remote(src.at[sxs, sys_, :], dst.at[dxs, dys, :], d)

    halos = [halo(perm, 0, 0, pm, d, 3) for d in DIRS]
    halos += [halo(accum, 0, 0, w, d, 2) for d in DIRS]
    halos += [halo(rhs, 0, 0, r, d, 2) for d in DIRS]
    halos += [remote(depth_y, hy.at[0], (1, 0)), remote(depth_y, hy.at[1], (-1, 0)),
              remote(depth_x, hx.at[0], (0, 1)), remote(depth_x, hx.at[1], (0, -1))]
    start(halos)

    for ref in (xb, xc):
        ref[0, 6:8] = jnp.zeros((2, ey, nz), jnp.float32)
        ref[1, 0:2] = jnp.zeros((2, ey, nz), jnp.float32)

    def clear(i):
        for ref in (yw, yb, yc):
            for u in range(2):
                ref[u, pl.ds(i * 2, 2)] = jnp.zeros((2, 16, nz), jnp.float32)
    each(ex // 2, clear)

    dx_ref[...] = jnp.zeros(dx_ref.shape, jnp.int32)
    dy_ref[...] = jnp.zeros(dy_ref.shape, jnp.int32)
    for side in range(2):
        dx_ref[side, own_y, :] = jnp.broadcast_to(depth_x[side:side + 1, :], (nz, by)).T
        lanes = jnp.broadcast_to(depth_y[side:side + 1, :], (nz, bx)).T
        dy_ref[side, own_x] = jnp.broadcast_to(lanes[:, None, :], (bx, 8, nz))

    def at(ref, x0, y0, rows=8, columns=8):
        return ref[pl.ds(x0, rows), pl.ds(y0, columns), :]

    def put(ref, x0, y0, value):
        ref[pl.ds(x0, value.shape[0]), pl.ds(y0, value.shape[1]), :] = value

    def strip_x(t):
        return PADX - 2 + t * (bx - 4)

    def strip_y(u):
        return PADY - 4 + u * (by - 8)

    def sublane(rows):
        return lax.broadcasted_iota(jnp.int32, (rows, 8, nz), 1)

    def stencil(ref, x0, y0, rows=8, following=None, lx=0, ly=0):
        wide = at(ref, x0 - lx - 1, y0 - ly, rows + 2)
        centre = wide[1:rows + 1]
        face = at(fx, x0 - 1, y0, rows + 1)
        total = face[0:rows] * wide[0:rows] + face[1:rows + 1] * wide[2:rows + 2]
        low = at(fy, x0, y0, rows)
        total = total + low * at(ref, x0 - lx, y0 - ly - 1, rows)
        back = pltpu.roll(low * centre, 7, 1)
        if following is None:
            total = total + at(fy, x0, y0 + 1, rows) * at(ref, x0 - lx, y0 - ly + 1, rows)
        else:
            total = total + jnp.where(sublane(rows) == 7, following, back)
        up = at(fz, x0, y0, rows)
        total = total + up * pltpu.roll(centre, nz - 1, 2)
        total = total + pltpu.roll(up * centre, 1, 2)
        return total, centre, back

    def coefficients(x0, y0, rows=8, following=None, frame=False):
        wide = 2.0 * at(pm, x0 - 1, y0, rows + 2)
        centre = wide[1:rows + 1]
        across_x = harmonic(wide[0:rows + 1], wide[1:rows + 2])
        across_y0 = harmonic(2.0 * at(pm, x0, y0 - 1, rows), centre)
        lane = lax.broadcasted_iota(jnp.int32, (1, 8, nz), 2)
        scale = jnp.where(lane < nz - 1, jnp.float32(VERTICAL), 0.0)
        up = scale * harmonic(centre, pltpu.roll(centre, nz - 1, 2))
        if following is None:
            across_y1 = harmonic(centre, 2.0 * at(pm, x0, y0 + 1, rows))
        else:
            across_y1 = pltpu.roll(jnp.where(sublane(rows) == 0, following, across_y0), 7, 1)
        if frame:
            row = x0 - 1 + lax.broadcasted_iota(jnp.int32, (rows + 1, 8, nz), 0)
            shut = (row == jnp.where(s == 0, PADX - 1, -1)) | (
                row == jnp.where(s == n_sub - 1, x_end - 1, -1))
            across_x = jnp.where(shut, 0.0, across_x)
            column = y0 + sublane(rows)
            first = jnp.where(k == 0, PADY, -1)
            last = jnp.where(k == n_col - 1, y_end, -1)
            across_y0 = jnp.where((column == first) | (column == last), 0.0, across_y0)
            across_y1 = jnp.where((column + 1 == first) | (column + 1 == last), 0.0, across_y1)
        put(fx, x0 - 1, y0, across_x)
        put(fy, x0, y0, across_y0)
        put(fz, x0, y0, up)
        faces = (across_x[0:rows] + across_x[1:rows + 1] + across_y0 + across_y1
                 + up + pltpu.roll(up, 1, 2))
        inverse = recip(at(w, x0, y0, rows) + faces)
        if not frame:
            put(w, x0, y0, inverse)
            put(b, x0, y0, inverse * at(r, x0, y0, rows))
        return inverse, across_y0

    def end_y(t, u):
        return jnp.where(t == 0, hy[0, pl.ds(u, 1), bx - 1:bx], hy[1, pl.ds(u, 1), 0:1])[None]

    def end_x(u, t):
        return jnp.where(u == 0, hx[0, pl.ds(t, 1), by - 1:by], hx[1, pl.ds(t, 1), 0:1])[None]

    def frame_block(x0, y0, rows, t, u, first):
        if first:
            inverse, _ = coefficients(x0, y0, rows, frame=True)
            i = x0 - PADX + lax.broadcasted_iota(jnp.int32, (rows, 8, nz), 0)
            j = y0 - PADY + sublane(rows)
            in_x, in_y = (i >= 0) & (i < bx), (j >= 0) & (j < by)
            member = in_x & in_y
            if t is not None:
                m = jnp.where(t == 0, i, bx - 1 - i)
                deep = dx_ref[t, pl.ds(y0, 8), :][None]
                member = member | ((m < 0) & (-1 - m < deep))
                other = ((m < 0) & in_y) | ((m >= 0) & (m < deep))
                if u is not None:
                    edge = end_y(t, u)
                    other = other | ((m == -1) & (j == jnp.where(u == 0, -1, by)) & (edge >= 1))
                weight_x = jnp.where(other, inverse, 0.0)
                put(xw.at[t], x0 - strip_x(t), y0, weight_x)
            if u is not None:
                m_y = jnp.where(u == 0, j, by - 1 - j)
                deep = dy_ref[u, pl.ds(x0, rows), :, :]
                member = member | ((m_y < 0) & (-1 - m_y < deep))
                other = ((m_y < 0) & in_x) | ((m_y >= 0) & (m_y < deep))
                if t is not None:
                    edge = end_x(u, t)
                    other = other | ((m_y == -1) & (i == jnp.where(t == 0, -1, bx)) & (edge >= 1))
                weight_y = jnp.where(other, inverse, 0.0)
                put(yw.at[u], x0, y0 - strip_y(u), weight_y)
            weight = jnp.where(member, inverse, 0.0)
            put(w, x0, y0, weight)
            source = at(r, x0, y0, rows)
            put(b, x0, y0, weight * source)
            if t is not None:
                put(xb.at[t], x0 - strip_x(t), y0, weight_x * source)
            if u is not None:
                put(yb.at[u], x0, y0 - strip_y(u), weight_y * source)
            return
        total, centre, _ = stencil(pr, x0, y0, rows)
        total = at(r, x0, y0, rows) + total

        def restarted(weight):
            return jnp.where(weight > 0.0, weight * total - centre, 0.0)

        put(b, x0, y0, restarted(at(w, x0, y0, rows)))
        if t is not None:
            lx = strip_x(t)
            put(xb.at[t], x0 - lx, y0, restarted(at(xw.at[t], x0 - lx, y0, rows)))
        if u is not None:
            ly = strip_y(u)
            put(yb.at[u], x0, y0 - ly, restarted(at(yw.at[u], x0, y0 - ly, rows)))

    def row(a):
        return PADX + 4 + 8 * a

    def column(q):
        return PADY - 4 + 8 * q

    def frame(first):
        unroll = 5 if (n_q - 2) % 5 == 0 else 1

        def along_x(n):
            t, q = n // ((n_q - 2) // unroll), n % ((n_q - 2) // unroll)
            for v in range(unroll):
                frame_block(PADX - 2 + t * (bx - 2), column(1 + q * unroll + v), 6, t, None, first)
        each(2 * ((n_q - 2) // unroll), along_x)

        def along_y(u):
            for a in range(n_a):
                frame_block(row(a), column(u * (n_q - 1)), 8, None, u, first)
        each(2, along_y)

        def corner(n):
            t, u = n // 2, n % 2
            frame_block(PADX - 2 + t * (bx - 2), column(u * (n_q - 1)), 6, t, u, first)
        each(4, corner)

    def chain(body, columns, *args):
        following = None
        for q in reversed(columns):
            following = body(*args, q, following)

    def second(x0, rows, q, following):
        y0 = column(q)
        total, _, back = stencil(b, x0, y0, rows, following)
        put(c, x0, y0, at(b, x0, y0, rows) + at(w, x0, y0, rows) * total)
        return back

    def second_inner():
        each(n_a - 2, lambda a: chain(second, range(2, n_q - 2), row(a + 1), 8))

    def second_outer():
        def ends(a):
            chain(second, range(n_q - 2, n_q), row(a + 1), 8)
            chain(second, range(0, 2), row(a + 1), 8)
        each(n_a - 2, ends)
        each(2, lambda t: chain(second, range(n_q), PADX + 4 + t * (bx - 16), 8))
        each(2, lambda t: chain(second, range(n_q), PADX - 1 + t * (bx - 3), 5))

    def second_strips():
        def along_x(t):
            lx = strip_x(t)
            x0 = PADX - 1 + t * (bx - 3)
            src, dst, weight = xb.at[t], xc.at[t], xw.at[t]

            def block(q, following):
                y0 = column(q)
                total, _, back = stencil(src, x0, y0, 5, following, lx, 0)
                put(dst, x0 - lx, y0, at(src, x0 - lx, y0, 5) + at(weight, x0 - lx, y0, 5) * total)
                return back
            chain(block, range(n_q))
        each(2, along_x)

        def along_y(u):
            ly = strip_y(u)
            y0 = PADY - 3 + u * (by - 2)
            src, dst, weight = yb.at[u], yc.at[u], yw.at[u]
            for a in range(bx // 8):
                x0 = PADX + 8 * a
                total, _, _ = stencil(src, x0, y0, 8, None, 0, ly)
                put(dst, x0, y0 - ly, at(src, x0, y0 - ly) + at(weight, x0, y0 - ly) * total)
        each(2, along_y)

    def finish(turn, x0, y0, value):
        if turn == 0:
            put(pr, x0, y0, value)
        else:
            put(out, x0 - PADX, y0 - PADY, at(pr, x0, y0, value.shape[0]) + value)

    def third(x0, y0, rows, following):
        total, _, back = stencil(c, x0, y0, rows, following)
        return at(b, x0, y0, rows) + at(w, x0, y0, rows) * total, back

    def third_inner(turn):
        def block(x0, q, following):
            y0 = PADY + 8 * q
            value, back = third(x0, y0, 8, following)
            finish(turn, x0, y0, value)
            return back
        each(n_a, lambda a: chain(block, range(1, by // 8 - 1), row(a)))

    def border(turn, x0, y0, rows, t, u, following=(None, None)):
        total, back = third(x0, y0, rows, following[0])
        cover = jnp.ones(total.shape, jnp.float32)
        back_x = None
        if t is not None:
            lx = strip_x(t)
            weight = at(xw.at[t], x0 - lx, y0, rows)
            others, _, back_x = stencil(xc.at[t], x0, y0, rows, following[1], lx, 0)
            total = total + (at(xb.at[t], x0 - lx, y0, rows) + weight * others)
            cover = jnp.where(weight > 0.0, cover + 1.0, cover)
        if u is not None:
            ly = strip_y(u)
            weight = at(yw.at[u], x0, y0 - ly, rows)
            others, _, _ = stencil(yc.at[u], x0, y0, rows, None, 0, ly)
            total = total + (at(yb.at[u], x0, y0 - ly, rows) + weight * others)
            cover = jnp.where(weight > 0.0, cover + 1.0, cover)
        finish(turn, x0, y0, total * recip(cover))
        return back, back_x

    def third_border(turn):
        def corner(n):
            t, u = n // 2, n % 2
            border(turn, PADX + t * (bx - 4), PADY + u * (by - 8), 4, t, u)
        each(4, corner)

        def along_x(t):
            following = (None, None)
            for q in reversed(range(1, by // 8 - 1)):
                following = border(turn, PADX + t * (bx - 4), PADY + 8 * q, 4, t, None, following)
        each(2, along_x)

        def along_y(u):
            for a in range(n_a):
                border(turn, row(a), PADY + u * (by - 8), 8, None, u)
        each(2, along_y)

    for copy in local(0):
        copy.wait()

    def first_row(a):
        for copy in local(a + 1):
            copy.wait()
        following = None
        for q in reversed(range(1, n_q - 1)):
            _, following = coefficients(row(a), column(q), following=following)
    each(n_a, first_row)
    second_inner()
    wait_recv(halos)
    frame(True)
    second_outer()
    second_strips()
    third_border(0)
    spread = [halo(pr, PADX, PADY, pr, d, 3) for d in DIRS]
    start(spread)
    third_inner(0)

    def restart_row(a):
        following = None
        for q in reversed(range(1, n_q - 1)):
            x0, y0 = row(a), column(q)
            total, centre, following = stencil(pr, x0, y0, 8, following)
            put(b, x0, y0, at(w, x0, y0) * (at(r, x0, y0) + total) - centre)
    each(n_a, restart_row)
    second_inner()
    wait_recv(spread)
    frame(False)
    second_outer()
    second_strips()
    third_border(1)
    third_inner(1)
    wait_send(halos)
    wait_send(spread)


def store(source, target, sem):
    rows = source.shape[0] // 8
    copies = [pltpu.make_async_copy(source.at[pl.ds(i * rows, rows)], target.at[pl.ds(i * rows, rows)], sem.at[i])
              for i in range(8)]
    for copy in copies:
        copy.start()
    for copy in copies:
        copy.wait()


def shards(n_sub, n_col, perm, accum, rhs, depth_x, depth_y):
    bx, by, nz = perm.shape
    ex, ey = bx + 2 * PADX, by + 2 * PADY
    field = pltpu.VMEM((ex, ey, nz), jnp.float32)
    strips_x = pltpu.VMEM((2, 8, ey, nz), jnp.float32)
    strips_y = pltpu.VMEM((2, ex, 16, nz), jnp.float32)
    hbm = pl.BlockSpec(memory_space=pl.ANY)
    vmem = pl.BlockSpec(memory_space=pltpu.VMEM)
    copies = 24 + 4 + 8
    result = pl.pallas_call(
        functools.partial(kernel, n_sub, n_col, bx, by),
        out_shape=pltpu.VMEM((bx, by, nz), jnp.float32),
        in_specs=[hbm, hbm, hbm, vmem, vmem],
        out_specs=vmem,
        scratch_shapes=[
            pltpu.VMEM((2, ey, nz), jnp.int32),
            pltpu.VMEM((2, ex, 8, nz), jnp.int32),
            pltpu.VMEM((2, 2, by), jnp.int32),
            pltpu.VMEM((2, 2, bx), jnp.int32),
        ] + [field] * 8 + [strips_x] * 3 + [strips_y] * 3 + [
            pltpu.SemaphoreType.DMA((copies,)),
            pltpu.SemaphoreType.DMA((copies,)),
            pltpu.SemaphoreType.DMA((3, bx // CHUNK)),
        ],
        compiler_params=pltpu.CompilerParams(
            collective_id=0, has_side_effects=True, vmem_limit_bytes=56 * 1024 * 1024),
        cost_estimate=pl.CostEstimate(
            flops=120 * bx * by * nz, bytes_accessed=16 * bx * by * nz, transcendentals=0),
    )(perm, accum, rhs, depth_x, depth_y.T)
    return pl.pallas_call(
        store,
        out_shape=jax.ShapeDtypeStruct((bx, by, nz), jnp.float32),
        in_specs=[vmem], out_specs=hbm,
        scratch_shapes=[pltpu.SemaphoreType.DMA((8,))],
        compiler_params=pltpu.CompilerParams(vmem_limit_bytes=4 * 1024 * 1024),
    )(result)


def solution(mesh):
    placed = (
        P("sub", "col", None),
        P("sub", "col", None),
        P("sub", "col", None),
        P("sub", "col"),
        P("sub", "col"),
    )
    return jax.shard_map(
        functools.partial(shards, mesh.shape["sub"], mesh.shape["col"]),
        mesh=mesh, in_specs=placed, out_specs=P("sub", "col", None), check_vma=False
    )
```

time: 63.7 us -> 43.4 us (0.68)
  Pallas kernels: 59.9 us -> 43.2 us
  local copies, waits for them, and re-layouts: 3.56 us -> 0 us
    pallas_call x1, Pallas kernels: 57.5 us -> 41.1 us  [shards(): pl.pallas_call(functools.partial(kernel, n_sub, n_col, bx, by), out_shape...]
    unnamed x3 -> x0, local copies, waits for them, and re-layouts: 3.56 us -> none
where the time goes in v1:
time: 43.4 us; the launch traced here: 43.2 us
  Pallas kernels  43.2 us (100%)
    pallas_call x1, Pallas kernels, shards(): pl.pallas_call(functools.partial(kernel, n_sub, n_col, bx, by), out_shape...  41.1 us
    pallas_call x1, Pallas kernels, shards(): pl.pallas_call(store, out_shape=jax.ShapeDtypeStruct((bx, by, nz), jnp.fl...  2.07 us

profile of v1, /device:TPU:19, one launch (start us, length us, event | category | flops | bytes accessed | tf_op | source)
XLA Modules:
  0.0 43.2 jit_solution(284561038080267498)
XLA Ops:
  0.0 41.1 %shard_map.55.source = f32[64,128,128]{2,1,0:T(8,128)S(1)} custom-call(f32[64,128,128]{2,1,0:T(8,128)} %perm.1, f32[64,128,128]{2,1,0:T(8,128)} %accum.1, f32[64,128,128]{2,1,0:T(8,128)} %rhs.1, s32[2,128]{1,0:T(2,128)} %depth_x.1, s32[2,64]{1,0:T(2,128)} %bitcast.1), custom_call_target="tpu_custom_call" | custom-call | flops 125829120 | bytes 16777216 | tf_op jit(solution)/shard_map/pallas_call | solution.py:457
  41.1 2.1 %shard_map.56 = f32[64,128,128]{2,1,0:T(8,128)} custom-call(f32[64,128,128]{2,1,0:T(8,128)S(1)} %shard_map.55.source), custom_call_target="tpu_custom_call" | custom-call | tf_op jit(solution)/shard_map/pallas_call | solution.py:477

commit v2 on v1

v2 whole, which is shorter than its diff:
```python
import functools

import jax
import jax.numpy as jnp
from jax import lax
from jax.experimental import pallas as pl
from jax.experimental.pallas import tpu as pltpu
from jax.sharding import PartitionSpec as P

OVL = 4
VERTICAL = 0.1
MESH = pl.DeviceIdType.MESH

PADX = 3
PADY = 8
DIRS = ((-1, 0), (1, 0), (0, -1), (0, 1), (-1, -1), (-1, 1), (1, -1), (1, 1))
CHUNK = 8


def recip(value):
    return pl.reciprocal(value, approx=True)


def harmonic(first, second):
    return first * second * recip(first + second)


def kernel(n_sub, n_col, bx, by, perm, accum, rhs, depth_x, depth_y, out,
           dx_ref, dy_ref, hx, hy, pm, w, r, b, fx, fy, fz, pr,
           xw, xb, xc, yw, yb, yc, ssem, rsem, lsem):
    nz = 128
    s = lax.axis_index("sub")
    k = lax.axis_index("col")
    ex, ey = bx + 2 * PADX, by + 2 * PADY
    c = pm
    n_a, n_q = bx // 8 - 1, by // 8 + 1
    x_end, y_end = PADX + bx, PADY + by

    def exists(d):
        ok = None
        for coord, step, count in ((s, d[0], n_sub), (k, d[1], n_col)):
            if step == -1:
                test = coord > 0
            elif step == 1:
                test = coord < count - 1
            else:
                continue
            ok = test if ok is None else ok & test
        return ok

    def device(d):
        return (s + d[0], k + d[1])

    own_x, own_y = pl.ds(PADX, bx), pl.ds(PADY, by)

    def local(n):
        here = pl.ds(n * CHUNK, CHUNK)
        there = pl.ds(PADX + n * CHUNK, CHUNK)
        return [pltpu.make_async_copy(src.at[here], dst.at[there, own_y, :], lsem.at[i, n])
                for i, (src, dst) in enumerate(((perm, pm), (accum, w), (rhs, r)))]

    for n in range(bx // CHUNK):
        for copy in local(n):
            copy.start()

    def each(count, body):
        def step(i, carry):
            body(i)
            return carry
        lax.fori_loop(0, count, step, 0)

    def fill(value, *refs):
        for ref in refs:
            for x0 in (0, x_end):
                ref[x0:x0 + PADX, :, :] = jnp.full((PADX, ey, nz), value, jnp.float32)

        def rows(i):
            for ref in refs:
                for y0 in (0, y_end):
                    ref[pl.ds(PADX + 8 * i, 8), y0:y0 + PADY, :] = jnp.full((8, PADY, nz), value, jnp.float32)
        each(bx // 8, rows)

    fill(1e-30, pm)
    fill(1.0, w)
    fill(0.0, r, pr)
    hx[...] = jnp.zeros(hx.shape, jnp.int32)
    hy[...] = jnp.zeros(hy.shape, jnp.int32)

    barrier = pltpu.get_barrier_semaphore()
    arrivals = jnp.int32(0)
    for d in DIRS:
        @pl.when(exists(d))
        def _(d=d):
            pl.semaphore_signal(barrier, inc=1, device_id=device(d), device_id_type=MESH)
        arrivals = arrivals + jnp.where(exists(d), 1, 0).astype(jnp.int32)
    pl.semaphore_wait(barrier, arrivals)

    counter = [0]

    def remote(src, dst, d):
        i = counter[0]
        counter[0] += 1
        return d, pltpu.make_async_remote_copy(
            src_ref=src, dst_ref=dst, send_sem=ssem.at[i], recv_sem=rsem.at[i],
            device_id=device(d), device_id_type=MESH)

    def start(copies):
        for d, copy in copies:
            pl.when(exists(d))(copy.start)

    def wait_recv(copies):
        for d, copy in copies:
            pl.when(exists((-d[0], -d[1])))(copy.wait_recv)

    def wait_send(copies):
        for d, copy in copies:
            pl.when(exists(d))(copy.wait_send)

    def halo(src, ox, oy, dst, d, width):
        def span(step, offset, extent, pad, thick):
            if step == 0:
                return pl.ds(offset, extent), pl.ds(pad, extent)
            if step == 1:
                return pl.ds(offset + extent - thick, thick), pl.ds(pad - thick, thick)
            return pl.ds(offset, thick), pl.ds(pad + extent, thick)

        sxs, dxs = span(d[0], ox, bx, PADX, width)
        sys_, dys = span(d[1], oy, by, PADY, width)
        return remote(src.at[sxs, sys_, :], dst.at[dxs, dys, :], d)

    halos = [halo(perm, 0, 0, pm, d, 3) for d in DIRS]
    halos += [halo(accum, 0, 0, w, d, 2) for d in DIRS]
    halos += [halo(rhs, 0, 0, r, d, 2) for d in DIRS]
    halos += [remote(depth_y, hy.at[0], (1, 0)), remote(depth_y, hy.at[1], (-1, 0)),
              remote(depth_x, hx.at[0], (0, 1)), remote(depth_x, hx.at[1], (0, -1))]
    start(halos)

    for ref in (xb, xc):
        ref[0, 6:8] = jnp.zeros((2, ey, nz), jnp.float32)
        ref[1, 0:2] = jnp.zeros((2, ey, nz), jnp.float32)

    def clear(i):
        for ref in (yw, yb, yc):
            for u in range(2):
                ref[u, pl.ds(i * 2, 2)] = jnp.zeros((2, 16, nz), jnp.float32)
    each(ex // 2, clear)

    dx_ref[...] = jnp.zeros(dx_ref.shape, jnp.int32)
    dy_ref[...] = jnp.zeros(dy_ref.shape, jnp.int32)
    for side in range(2):
        dx_ref[side, own_y, :] = jnp.broadcast_to(depth_x[side:side + 1, :], (nz, by)).T
        lanes = jnp.broadcast_to(depth_y[side:side + 1, :], (nz, bx)).T
        dy_ref[side, own_x] = jnp.broadcast_to(lanes[:, None, :], (bx, 8, nz))

    def at(ref, x, y0):
        return ref[x, pl.ds(y0, 8), :]

    def put(ref, x, y0, value):
        ref[x, pl.ds(y0, 8), :] = value

    def strip_x(t):
        return PADX - 2 + t * (bx - 4)

    def strip_y(u):
        return PADY - 4 + u * (by - 8)

    sublane = lax.broadcasted_iota(jnp.int32, (8, nz), 0)
    lane = lax.broadcasted_iota(jnp.int32, (8, nz), 1)

    def stencil(ref, x0, y0, rows, emit, following=None, lx=0, ly=0):
        before, centre = at(ref, x0 - lx - 1, y0 - ly), at(ref, x0 - lx, y0 - ly)
        face = at(fx, x0 - 1, y0)
        backs = []
        for i in range(rows):
            x = x0 + i
            after = at(ref, x - lx + 1, y0 - ly)
            total = face * before
            face = at(fx, x, y0)
            total = total + face * after
            low = at(fy, x, y0)
            total = total + low * at(ref, x - lx, y0 - ly - 1)
            back = pltpu.roll(low * centre, 7, 0)
            if following is None:
                total = total + at(fy, x, y0 + 1) * at(ref, x - lx, y0 - ly + 1)
            else:
                total = total + jnp.where(sublane == 7, following[i], back)
            up = at(fz, x, y0)
            total = total + up * pltpu.roll(centre, nz - 1, 1)
            total = total + pltpu.roll(up * centre, 1, 1)
            emit(i, total, centre)
            backs.append(back)
            before, centre = centre, after
        return backs

    def coefficients(x0, y0, rows, emit, following=None):
        before, centre = 2.0 * at(pm, x0 - 1, y0), 2.0 * at(pm, x0, y0)
        face = harmonic(before, centre)
        put(fx, x0 - 1, y0, face)
        lows = []
        for i in range(rows):
            x = x0 + i
            after = 2.0 * at(pm, x + 1, y0)
            faces = face
            face = harmonic(centre, after)
            put(fx, x, y0, face)
            faces = faces + face
            low = harmonic(2.0 * at(pm, x, y0 - 1), centre)
            put(fy, x, y0, low)
            if following is None:
                high = harmonic(centre, 2.0 * at(pm, x, y0 + 1))
            else:
                high = pltpu.roll(jnp.where(sublane == 0, following[i], low), 7, 0)
            faces = faces + low + high
            scale = jnp.where(lane < nz - 1, jnp.float32(VERTICAL), 0.0)
            up = scale * harmonic(centre, pltpu.roll(centre, nz - 1, 1))
            put(fz, x, y0, up)
            faces = faces + up + pltpu.roll(up, 1, 1)
            emit(i, recip(at(w, x, y0) + faces))
            lows.append(low)
            centre = after
        return lows

    def end_y(t, u):
        return jnp.where(t == 0, hy[0, pl.ds(u, 1), bx - 1:bx], hy[1, pl.ds(u, 1), 0:1])

    def end_x(u, t):
        return jnp.where(u == 0, hx[0, pl.ds(t, 1), by - 1:by], hx[1, pl.ds(t, 1), 0:1])

    def strips(x0, y0, t, u):
        found = []
        if t is not None:
            found.append((xw.at[t], xb.at[t], x0 - strip_x(t), y0))
        if u is not None:
            found.append((yw.at[u], yb.at[u], x0, y0 - strip_y(u)))
        return found

    def frame_first(x0, y0, rows, t, u):
        j = y0 - PADY + sublane
        in_y = (j >= 0) & (j < by)
        if t is not None:
            deep_x = dx_ref[t, pl.ds(y0, 8), :]
        if u is not None:
            m_y = jnp.where(u == 0, j, by - 1 - j)
        if t is not None and u is not None:
            corner_x = (m_y == -1) & (end_y(t, u) >= 1)
            corner_y = (m_y == -1) & (end_x(u, t) >= 1)

        def emit(n, inverse):
            x = x0 + n
            i = x - PADX
            source = at(r, x, y0)
            if t is None:
                member = in_y
            else:
                m = jnp.where(t == 0, i, bx - 1 - i)
                beyond = m < 0
                member = jnp.where(beyond, -1 - m, jnp.where(in_y, -1, 8)) < deep_x
                other = jnp.where(beyond, jnp.where(in_y, -1, 8), m) < deep_x
                if u is not None:
                    other = other | (corner_x & (m == -1))
                weight = jnp.where(other, inverse, 0.0)
                put(xw.at[t], x - strip_x(t), y0, weight)
                put(xb.at[t], x - strip_x(t), y0, weight * source)
            if u is not None:
                deep_y = dy_ref[u, x]
                inside = jnp.where((i >= 0) & (i < bx), 0, 8)
                member = member | (jnp.where(m_y < 0, -1 - m_y, 8) < deep_y)
                other = jnp.where(m_y < 0, inside - 1, m_y) < deep_y
                if t is not None:
                    other = other | (corner_y & (m == -1))
                weight = jnp.where(other, inverse, 0.0)
                put(yw.at[u], x, y0 - strip_y(u), weight)
                put(yb.at[u], x, y0 - strip_y(u), weight * source)
            weight = jnp.where(member, inverse, 0.0)
            put(w, x, y0, weight)
            put(b, x, y0, weight * source)
        coefficients(x0, y0, rows, emit)

    def frame_again(x0, y0, rows, t, u):
        def emit(n, total, centre):
            x = x0 + n
            total = at(r, x, y0) + total
            for weights, target, x1, y1 in [(w, b, x0, y0)] + strips(x0, y0, t, u):
                weight = at(weights, x1 + n, y1)
                put(target, x1 + n, y1, jnp.where(weight > 0.0, weight * total - centre, 0.0))
        stencil(pr, x0, y0, rows, emit)

    def row(a):
        return PADX + 4 + 8 * a

    def column(q):
        return PADY - 4 + 8 * q

    def frame(block):
        unroll = 5 if (n_q - 2) % 5 == 0 else 1

        def along_x(n):
            t, q = n // ((n_q - 2) // unroll), n % ((n_q - 2) // unroll)
            for v in range(unroll):
                block(PADX - 2 + t * (bx - 2), column(1 + q * unroll + v), 6, t, None)
        each(2 * ((n_q - 2) // unroll), along_x)

        def along_y(u):
            for a in range(n_a):
                block(row(a), column(u * (n_q - 1)), 8, None, u)
        each(2, along_y)

        def corner(n):
            t, u = n // 2, n % 2
            block(PADX - 2 + t * (bx - 2), column(u * (n_q - 1)), 6, t, u)
        each(4, corner)

    def chain(body, columns, *args):
        following = None
        for q in reversed(columns):
            following = body(*args, q, following)

    def second(x0, rows, q, following):
        y0 = column(q)

        def emit(i, total, centre):
            put(c, x0 + i, y0, centre + at(w, x0 + i, y0) * total)
        return stencil(b, x0, y0, rows, emit, following)

    def second_inner():
        each(n_a - 2, lambda a: chain(second, range(2, n_q - 2), row(a + 1), 8))

    def second_outer():
        def ends(a):
            chain(second, range(n_q - 2, n_q), row(a + 1), 8)
            chain(second, range(0, 2), row(a + 1), 8)
        each(n_a - 2, ends)
        each(2, lambda t: chain(second, range(n_q), PADX + 4 + t * (bx - 16), 8))
        each(2, lambda t: chain(second, range(n_q), PADX - 1 + t * (bx - 3), 5))

    def second_strips():
        def strip(src, dst, weight, x0, y0, rows, following, lx, ly):
            def emit(i, total, centre):
                x, y = x0 - lx + i, y0 - ly
                put(dst, x, y, centre + at(weight, x, y) * total)
            return stencil(src, x0, y0, rows, emit, following, lx, ly)

        def along_x(t):
            def block(q, following):
                return strip(xb.at[t], xc.at[t], xw.at[t], PADX - 1 + t * (bx - 3), column(q), 5, following, strip_x(t), 0)
            chain(block, range(n_q))
        each(2, along_x)

        def along_y(u):
            for a in range(bx // 8):
                strip(yb.at[u], yc.at[u], yw.at[u], PADX + 8 * a, PADY - 3 + u * (by - 2), 8, None, 0, strip_y(u))
        each(2, along_y)

    def finish(turn, x, y0, value):
        if turn == 0:
            put(pr, x, y0, value)
        else:
            put(out, x - PADX, y0 - PADY, at(pr, x, y0) + value)

    def third_inner(turn):
        def block(x0, q, following):
            y0 = PADY + 8 * q

            def emit(i, total, centre):
                x = x0 + i
                finish(turn, x, y0, at(b, x, y0) + at(w, x, y0) * total)
            return stencil(c, x0, y0, 8, emit, following)
        each(n_a, lambda a: chain(block, range(1, by // 8 - 1), row(a)))

    def border(turn, x0, y0, rows, t, u, following=(None, None)):
        sums, covers, backs = [None] * rows, [None] * rows, []

        def add(i, value, weight):
            sums[i] = value if sums[i] is None else sums[i] + value
            if weight is not None:
                covers[i] = jnp.where(weight > 0.0, 2.0 if covers[i] is None else covers[i] + 1.0,
                                      1.0 if covers[i] is None else covers[i])

        def own(i, total, centre):
            add(i, at(b, x0 + i, y0) + at(w, x0 + i, y0) * total, None)
        backs.append(stencil(c, x0, y0, rows, own, following[0]))
        for n, (weights, source, x1, y1) in enumerate(strips(x0, y0, t, u)):
            def other(i, total, centre, weights=weights, source=source, x1=x1, y1=y1):
                weight = at(weights, x1 + i, y1)
                add(i, at(source, x1 + i, y1) + weight * total, weight)
            along_x = t is not None and n == 0
            backs.append(stencil(xc.at[t] if along_x else yc.at[u], x0, y0, rows, other,
                                 following[1] if along_x else None, x0 - x1, y0 - y1))
        for i in range(rows):
            finish(turn, x0 + i, y0, sums[i] * recip(covers[i]))
        return backs

    def third_border(turn):
        def corner(n):
            t, u = n // 2, n % 2
            border(turn, PADX + t * (bx - 4), PADY + u * (by - 8), 4, t, u)
        each(4, corner)

        def along_x(t):
            following = (None, None)
            for q in reversed(range(1, by // 8 - 1)):
                following = border(turn, PADX + t * (bx - 4), PADY + 8 * q, 4, t, None, following)
        each(2, along_x)

        def along_y(u):
            for a in range(n_a):
                border(turn, row(a), PADY + u * (by - 8), 8, None, u)
        each(2, along_y)

    for copy in local(0):
        copy.wait()

    def first_row(a):
        for copy in local(a + 1):
            copy.wait()

        def block(x0, q, following):
            y0 = column(q)

            def emit(i, inverse):
                put(w, x0 + i, y0, inverse)
                put(b, x0 + i, y0, inverse * at(r, x0 + i, y0))
            return coefficients(x0, y0, 8, emit, following)
        chain(block, range(1, n_q - 1), row(a))
    each(n_a, first_row)
    second_inner()
    wait_recv(halos)
    frame(frame_first)
    second_outer()
    second_strips()
    third_border(0)
    spread = [halo(pr, PADX, PADY, pr, d, 3) for d in DIRS]
    start(spread)
    third_inner(0)

    def restart(x0, q, following):
        y0 = column(q)

        def emit(i, total, centre):
            x = x0 + i
            put(b, x, y0, at(w, x, y0) * (at(r, x, y0) + total) - centre)
        return stencil(pr, x0, y0, 8, emit, following)
    each(n_a, lambda a: chain(restart, range(1, n_q - 1), row(a)))
    second_inner()
    wait_recv(spread)
    frame(frame_again)
    second_outer()
    second_strips()
    third_border(1)
    third_inner(1)
    wait_send(halos)
    wait_send(spread)


def store(source, target, sem):
    rows = source.shape[0] // 8
    copies = [pltpu.make_async_copy(source.at[pl.ds(i * rows, rows)], target.at[pl.ds(i * rows, rows)], sem.at[i])
              for i in range(8)]
    for copy in copies:
        copy.start()
    for copy in copies:
        copy.wait()


def shards(n_sub, n_col, perm, accum, rhs, depth_x, depth_y):
    bx, by, nz = perm.shape
    ex, ey = bx + 2 * PADX, by + 2 * PADY
    field = pltpu.VMEM((ex, ey, nz), jnp.float32)
    strips_x = pltpu.VMEM((2, 8, ey, nz), jnp.float32)
    strips_y = pltpu.VMEM((2, ex, 16, nz), jnp.float32)
    hbm = pl.BlockSpec(memory_space=pl.ANY)
    vmem = pl.BlockSpec(memory_space=pltpu.VMEM)
    copies = 24 + 4 + 8
    result = pl.pallas_call(
        functools.partial(kernel, n_sub, n_col, bx, by),
        out_shape=pltpu.VMEM((bx, by, nz), jnp.float32),
        in_specs=[hbm, hbm, hbm, vmem, vmem],
        out_specs=vmem,
        scratch_shapes=[
            pltpu.VMEM((2, ey, nz), jnp.int32),
            pltpu.VMEM((2, ex, 8, nz), jnp.int32),
            pltpu.VMEM((2, 2, by), jnp.int32),
            pltpu.VMEM((2, 2, bx), jnp.int32),
        ] + [field] * 8 + [strips_x] * 3 + [strips_y] * 3 + [
            pltpu.SemaphoreType.DMA((copies,)),
            pltpu.SemaphoreType.DMA((copies,)),
            pltpu.SemaphoreType.DMA((3, bx // CHUNK)),
        ],
        compiler_params=pltpu.CompilerParams(
            collective_id=0, has_side_effects=True, vmem_limit_bytes=56 * 1024 * 1024),
        cost_estimate=pl.CostEstimate(
            flops=120 * bx * by * nz, bytes_accessed=16 * bx * by * nz, transcendentals=0),
    )(perm, accum, rhs, depth_x, depth_y.T)
    return pl.pallas_call(
        store,
        out_shape=jax.ShapeDtypeStruct((bx, by, nz), jnp.float32),
        in_specs=[vmem], out_specs=hbm,
        scratch_shapes=[pltpu.SemaphoreType.DMA((8,))],
        compiler_params=pltpu.CompilerParams(vmem_limit_bytes=4 * 1024 * 1024),
    )(result)


def solution(mesh):
    placed = (
        P("sub", "col", None),
        P("sub", "col", None),
        P("sub", "col", None),
        P("sub", "col"),
        P("sub", "col"),
    )
    return jax.shard_map(
        functools.partial(shards, mesh.shape["sub"], mesh.shape["col"]),
        mesh=mesh, in_specs=placed, out_specs=P("sub", "col", None), check_vma=False
    )
```

time: 43.4 us -> 42.7 us (0.984)
  Pallas kernels: 43.2 us -> 42.5 us
    pallas_call x1, Pallas kernels: 41.1 us -> 40.4 us  [shards(): pl.pallas_call(functools.partial(kernel, n_sub, n_col, bx, by), out_shape...]
where the time goes in v2:
time: 42.7 us; the launch traced here: 42.5 us
  Pallas kernels  42.5 us (100%)
    pallas_call x1, Pallas kernels, shards(): pl.pallas_call(functools.partial(kernel, n_sub, n_col, bx, by), out_shape...  40.4 us
    pallas_call x1, Pallas kernels, shards(): pl.pallas_call(store, out_shape=jax.ShapeDtypeStruct((bx, by, nz), jnp.fl...  2.07 us

profile of v2, /device:TPU:19, one launch (start us, length us, event | category | flops | bytes accessed | tf_op | source)
XLA Modules:
  0.0 42.5 jit_solution(9949705027853022813)
XLA Ops:
  0.0 40.4 %shard_map.55.source = f32[64,128,128]{2,1,0:T(8,128)S(1)} custom-call(f32[64,128,128]{2,1,0:T(8,128)} %perm.1, f32[64,128,128]{2,1,0:T(8,128)} %accum.1, f32[64,128,128]{2,1,0:T(8,128)} %rhs.1, s32[2,128]{1,0:T(2,128)} %depth_x.1, s32[2,64]{1,0:T(2,128)} %bitcast.1), custom_call_target="tpu_custom_call" | custom-call | flops 125829120 | bytes 16777216 | tf_op jit(solution)/shard_map/pallas_call | solution.py:474
  40.5 2.1 %shard_map.56 = f32[64,128,128]{2,1,0:T(8,128)} custom-call(f32[64,128,128]{2,1,0:T(8,128)S(1)} %shard_map.55.source), custom_call_target="tpu_custom_call" | custom-call | tf_op jit(solution)/shard_map/pallas_call | solution.py:494

commit v3 on v2

--- a/solution.py
+++ b/solution.py
@@ -26,8 +26,8 @@
 
 
 def kernel(n_sub, n_col, bx, by, perm, accum, rhs, depth_x, depth_y, out,
-           dx_ref, dy_ref, hx, hy, pm, w, r, b, fx, fy, fz, pr,
-           xw, xb, xc, yw, yb, yc, ssem, rsem, lsem):
+           dx_ref, dy_ref, kx, ky, hx, hy, pm, w, r, b, fx, fy, fz, pr,
+           xw, xb, xc, yw, yb, yc, ssem, rsem, lsem, dsem):
     nz = 128
     s = lax.axis_index("sub")
     k = lax.axis_index("col")
@@ -59,15 +59,19 @@
         return [pltpu.make_async_copy(src.at[here], dst.at[there, own_y, :], lsem.at[i, n])
                 for i, (src, dst) in enumerate(((perm, pm), (accum, w), (rhs, r)))]
 
+    depths = [pltpu.make_async_copy(depth_x, kx, dsem.at[0]), pltpu.make_async_copy(depth_y, ky, dsem.at[1])]
     for n in range(bx // CHUNK):
         for copy in local(n):
             copy.start()
-
-    def each(count, body):
+        if n == 0:
+            for copy in depths:
+                copy.start()
+
+    def each(count, body, first=0):
         def step(i, carry):
             body(i)
             return carry
-        lax.fori_loop(0, count, step, 0)
+        lax.fori_loop(first, count, step, 0)
 
     def fill(value, *refs):
         for ref in refs:
@@ -128,12 +132,16 @@
         sys_, dys = span(d[1], oy, by, PADY, width)
         return remote(src.at[sxs, sys_, :], dst.at[dxs, dys, :], d)
 
-    halos = [halo(perm, 0, 0, pm, d, 3) for d in DIRS]
-    halos += [halo(accum, 0, 0, w, d, 2) for d in DIRS]
-    halos += [halo(rhs, 0, 0, r, d, 2) for d in DIRS]
-    halos += [remote(depth_y, hy.at[0], (1, 0)), remote(depth_y, hy.at[1], (-1, 0)),
-              remote(depth_x, hx.at[0], (0, 1)), remote(depth_x, hx.at[1], (0, -1))]
-    start(halos)
+    def given(d):
+        return [halo(perm, 0, 0, pm, d, 3), halo(accum, 0, 0, w, d, 2), halo(rhs, 0, 0, r, d, 2)]
+
+    halos_x = [copy for pair in zip(given(DIRS[0]), given(DIRS[1])) for copy in pair]
+    halos_y = [copy for pair in zip(given(DIRS[2]), given(DIRS[3])) for copy in pair]
+    halos_x += [remote(depth_y, hy.at[0], (1, 0)), remote(depth_y, hy.at[1], (-1, 0)),
+                remote(depth_x, hx.at[0], (0, 1)), remote(depth_x, hx.at[1], (0, -1))]
+    halos_x += [copy for d in DIRS[4:] for copy in given(d)]
+    start(halos_y)
+    start(halos_x)
 
     for ref in (xb, xc):
         ref[0, 6:8] = jnp.zeros((2, ey, nz), jnp.float32)
@@ -142,14 +150,19 @@
     def clear(i):
         for ref in (yw, yb, yc):
             for u in range(2):
-                ref[u, pl.ds(i * 2, 2)] = jnp.zeros((2, 16, nz), jnp.float32)
-    each(ex // 2, clear)
-
+                ref[u, pl.ds(i * 10, 10), 8 - 8 * u:16 - 8 * u] = jnp.zeros((10, 8, nz), jnp.float32)
+    each(ex // 10, clear)
+    for u in range(2):
+        for x in (PADX - 1, x_end):
+            yc[u, x] = jnp.zeros((16, nz), jnp.float32)
+
+    for copy in depths:
+        copy.wait()
     dx_ref[...] = jnp.zeros(dx_ref.shape, jnp.int32)
     dy_ref[...] = jnp.zeros(dy_ref.shape, jnp.int32)
     for side in range(2):
-        dx_ref[side, own_y, :] = jnp.broadcast_to(depth_x[side:side + 1, :], (nz, by)).T
-        lanes = jnp.broadcast_to(depth_y[side:side + 1, :], (nz, bx)).T
+        dx_ref[side, own_y, :] = jnp.broadcast_to(kx[side:side + 1, :], (nz, by)).T
+        lanes = jnp.broadcast_to(ky[side:side + 1, :], (nz, bx)).T
         dy_ref[side, own_x] = jnp.broadcast_to(lanes[:, None, :], (bx, 8, nz))
 
     def at(ref, x, y0):
@@ -291,7 +304,7 @@
     def column(q):
         return PADY - 4 + 8 * q
 
-    def frame(block):
+    def frame_x(block):
         unroll = 5 if (n_q - 2) % 5 == 0 else 1
 
         def along_x(n):
@@ -300,16 +313,17 @@
                 block(PADX - 2 + t * (bx - 2), column(1 + q * unroll + v), 6, t, None)
         each(2 * ((n_q - 2) // unroll), along_x)
 
+        def corner(n):
+            t, u = n // 2, n % 2
+            block(PADX - 2 + t * (bx - 2), column(u * (n_q - 1)), 6, t, u)
+        each(4, corner)
+
+    def frame_y(block):
         def along_y(u):
             for a in range(n_a):
                 block(row(a), column(u * (n_q - 1)), 8, None, u)
         each(2, along_y)
 
-        def corner(n):
-            t, u = n // 2, n % 2
-            block(PADX - 2 + t * (bx - 2), column(u * (n_q - 1)), 6, t, u)
-        each(4, corner)
-
     def chain(body, columns, *args):
         following = None
         for q in reversed(columns):
@@ -325,29 +339,32 @@
     def second_inner():
         each(n_a - 2, lambda a: chain(second, range(2, n_q - 2), row(a + 1), 8))
 
-    def second_outer():
+    def second_ends():
         def ends(a):
             chain(second, range(n_q - 2, n_q), row(a + 1), 8)
             chain(second, range(0, 2), row(a + 1), 8)
         each(n_a - 2, ends)
+
+    def second_rows():
         each(2, lambda t: chain(second, range(n_q), PADX + 4 + t * (bx - 16), 8))
         each(2, lambda t: chain(second, range(n_q), PADX - 1 + t * (bx - 3), 5))
 
-    def second_strips():
-        def strip(src, dst, weight, x0, y0, rows, following, lx, ly):
-            def emit(i, total, centre):
-                x, y = x0 - lx + i, y0 - ly
-                put(dst, x, y, centre + at(weight, x, y) * total)
-            return stencil(src, x0, y0, rows, emit, following, lx, ly)
-
+    def strip(src, dst, weight, x0, y0, rows, following, lx, ly):
+        def emit(i, total, centre):
+            x, y = x0 - lx + i, y0 - ly
+            put(dst, x, y, centre + at(weight, x, y) * total)
+        return stencil(src, x0, y0, rows, emit, following, lx, ly)
+
+    def strips_along_x():
         def along_x(t):
             def block(q, following):
                 return strip(xb.at[t], xc.at[t], xw.at[t], PADX - 1 + t * (bx - 3), column(q), 5, following, strip_x(t), 0)
             chain(block, range(n_q))
         each(2, along_x)
 
+    def strips_along_y(*rows):
         def along_y(u):
-            for a in range(bx // 8):
+            for a in rows:
                 strip(yb.at[u], yc.at[u], yw.at[u], PADX + 8 * a, PADY - 3 + u * (by - 2), 8, None, 0, strip_y(u))
         each(2, along_y)
 
@@ -365,7 +382,7 @@
                 x = x0 + i
                 finish(turn, x, y0, at(b, x, y0) + at(w, x, y0) * total)
             return stencil(c, x0, y0, 8, emit, following)
-        each(n_a, lambda a: chain(block, range(1, by // 8 - 1), row(a)))
+        return lambda a: chain(block, range(1, by // 8 - 1), row(a))
 
     def border(turn, x0, y0, rows, t, u, following=(None, None)):
         sums, covers, backs = [None] * rows, [None] * rows, []
@@ -390,7 +407,7 @@
             finish(turn, x0 + i, y0, sums[i] * recip(covers[i]))
         return backs
 
-    def third_border(turn):
+    def border_x(turn):
         def corner(n):
             t, u = n // 2, n % 2
             border(turn, PADX + t * (bx - 4), PADY + u * (by - 8), 4, t, u)
@@ -402,8 +419,9 @@
                 following = border(turn, PADX + t * (bx - 4), PADY + 8 * q, 4, t, None, following)
         each(2, along_x)
 
+    def border_y(turn, *rows):
         def along_y(u):
-            for a in range(n_a):
+            for a in rows:
                 border(turn, row(a), PADY + u * (by - 8), 8, None, u)
         each(2, along_y)
 
@@ -423,15 +441,32 @@
             return coefficients(x0, y0, 8, emit, following)
         chain(block, range(1, n_q - 1), row(a))
     each(n_a, first_row)
-    second_inner()
-    wait_recv(halos)
-    frame(frame_first)
-    second_outer()
-    second_strips()
-    third_border(0)
-    spread = [halo(pr, PADX, PADY, pr, d, 3) for d in DIRS]
+    middle = range(2, n_a - 2)
+    ends = [a for a in range(n_a) if a not in middle]
+
+    def correct(turn, frame, along_y, along_x):
+        second_inner()
+        wait_recv(along_y)
+        frame_y(frame)
+        second_ends()
+        strips_along_y(*range(1, bx // 8 - 1))
+        border_y(turn, *middle)
+        each(n_a - 2, third_inner(turn), 2)
+        wait_recv(along_x)
+        frame_x(frame)
+        second_rows()
+        strips_along_x()
+        strips_along_y(0, bx // 8 - 1)
+        border_x(turn)
+        border_y(turn, *ends)
+
+    def third_ends(turn):
+        each(4, lambda n: third_inner(turn)(n + (n // 2) * (n_a - 4)))
+
+    correct(0, frame_first, halos_y, halos_x)
+    spread = [halo(pr, PADX, PADY, pr, d, 3) for d in (*DIRS[2:4], *DIRS[0:2], *DIRS[4:])]
     start(spread)
-    third_inner(0)
+    third_ends(0)
 
     def restart(x0, q, following):
         y0 = column(q)
@@ -441,14 +476,10 @@
             put(b, x, y0, at(w, x, y0) * (at(r, x, y0) + total) - centre)
         return stencil(pr, x0, y0, 8, emit, following)
     each(n_a, lambda a: chain(restart, range(1, n_q - 1), row(a)))
-    second_inner()
-    wait_recv(spread)
-    frame(frame_again)
-    second_outer()
-    second_strips()
-    third_border(1)
-    third_inner(1)
-    wait_send(halos)
+    correct(1, frame_again, spread[:2], spread[2:])
+    third_ends(1)
+    wait_send(halos_y)
+    wait_send(halos_x)
     wait_send(spread)
 
 
@@ -474,17 +505,20 @@
     result = pl.pallas_call(
         functools.partial(kernel, n_sub, n_col, bx, by),
         out_shape=pltpu.VMEM((bx, by, nz), jnp.float32),
-        in_specs=[hbm, hbm, hbm, vmem, vmem],
+        in_specs=[hbm] * 5,
         out_specs=vmem,
         scratch_shapes=[
             pltpu.VMEM((2, ey, nz), jnp.int32),
             pltpu.VMEM((2, ex, 8, nz), jnp.int32),
+            pltpu.VMEM((2, by), jnp.int32),
+            pltpu.VMEM((2, bx), jnp.int32),
             pltpu.VMEM((2, 2, by), jnp.int32),
             pltpu.VMEM((2, 2, bx), jnp.int32),
         ] + [field] * 8 + [strips_x] * 3 + [strips_y] * 3 + [
             pltpu.SemaphoreType.DMA((copies,)),
             pltpu.SemaphoreType.DMA((copies,)),
             pltpu.SemaphoreType.DMA((3, bx // CHUNK)),
+            pltpu.SemaphoreType.DMA((2,)),
         ],
         compiler_params=pltpu.CompilerParams(
             collective_id=0, has_side_effects=True, vmem_limit_bytes=56 * 1024 * 1024),

time: 42.7 us -> 39.7 us (0.930)
  Pallas kernels: 42.5 us -> 39.5 us
    pallas_call x1, Pallas kernels: 40.4 us -> 37.5 us  [shards(): pl.pallas_call(functools.partial(kernel, n_sub, n_col, bx, by), out_shape...]
where the time goes in v3:
time: 39.7 us; the launch traced here: 39.5 us
  Pallas kernels  39.5 us (99%)
    pallas_call x1, Pallas kernels, shards(): pl.pallas_call(functools.partial(kernel, n_sub, n_col, bx, by), out_shape...  37.5 us
    pallas_call x1, Pallas kernels, shards(): pl.pallas_call(store, out_shape=jax.ShapeDtypeStruct((bx, by, nz), jnp.fl...  2.07 us

profile of v3, /device:TPU:19, one launch (start us, length us, event | category | flops | bytes accessed | tf_op | source)
XLA Modules:
  0.0 39.5 jit_solution(1321948225106531172)
XLA Ops:
  0.0 37.5 %shard_map.55.source = f32[64,128,128]{2,1,0:T(8,128)S(1)} custom-call(f32[64,128,128]{2,1,0:T(8,128)} %perm.1, f32[64,128,128]{2,1,0:T(8,128)} %accum.1, f32[64,128,128]{2,1,0:T(8,128)} %rhs.1, s32[2,128]{1,0:T(2,128)} %depth_x.1, s32[2,64]{1,0:T(2,128)} %bitcast.1), custom_call_target="tpu_custom_call" | custom-call | flops 125829120 | bytes 16777216 | tf_op jit(solution)/shard_map/pallas_call | solution.py:505
  37.5 2.1 %shard_map.56 = f32[64,128,128]{2,1,0:T(8,128)} custom-call(f32[64,128,128]{2,1,0:T(8,128)S(1)} %shard_map.55.source), custom_call_target="tpu_custom_call" | custom-call | tf_op jit(solution)/shard_map/pallas_call | solution.py:528

commit v4 on v3

--- a/solution.py
+++ b/solution.py
@@ -97,8 +97,6 @@
         def _(d=d):
             pl.semaphore_signal(barrier, inc=1, device_id=device(d), device_id_type=MESH)
         arrivals = arrivals + jnp.where(exists(d), 1, 0).astype(jnp.int32)
-    pl.semaphore_wait(barrier, arrivals)
-
     counter = [0]
 
     def remote(src, dst, d):
@@ -140,8 +138,11 @@
     halos_x += [remote(depth_y, hy.at[0], (1, 0)), remote(depth_y, hy.at[1], (-1, 0)),
                 remote(depth_x, hx.at[0], (0, 1)), remote(depth_x, hx.at[1], (0, -1))]
     halos_x += [copy for d in DIRS[4:] for copy in given(d)]
-    start(halos_y)
-    start(halos_x)
+
+    def greet():
+        pl.semaphore_wait(barrier, arrivals)
+        start(halos_y)
+        start(halos_x)
 
     for ref in (xb, xc):
         ref[0, 6:8] = jnp.zeros((2, ey, nz), jnp.float32)
@@ -336,8 +337,8 @@
             put(c, x0 + i, y0, centre + at(w, x0 + i, y0) * total)
         return stencil(b, x0, y0, rows, emit, following)
 
-    def second_inner():
-        each(n_a - 2, lambda a: chain(second, range(2, n_q - 2), row(a + 1), 8))
+    def second_row(a):
+        chain(second, range(2, n_q - 2), row(a), 8)
 
     def second_ends():
         def ends(a):
@@ -374,15 +375,15 @@
         else:
             put(out, x - PADX, y0 - PADY, at(pr, x, y0) + value)
 
-    def third_inner(turn):
-        def block(x0, q, following):
+    def third_rows(turn, x0, rows):
+        def block(q, following):
             y0 = PADY + 8 * q
 
             def emit(i, total, centre):
                 x = x0 + i
                 finish(turn, x, y0, at(b, x, y0) + at(w, x, y0) * total)
-            return stencil(c, x0, y0, 8, emit, following)
-        return lambda a: chain(block, range(1, by // 8 - 1), row(a))
+            return stencil(c, x0, y0, rows, emit, following)
+        chain(block, range(1, by // 8 - 1))
 
     def border(turn, x0, y0, rows, t, u, following=(None, None)):
         sums, covers, backs = [None] * rows, [None] * rows, []
@@ -419,10 +420,10 @@
                 following = border(turn, PADX + t * (bx - 4), PADY + 8 * q, 4, t, None, following)
         each(2, along_x)
 
-    def border_y(turn, *rows):
+    def border_y(turn, *spans):
         def along_y(u):
-            for a in rows:
-                border(turn, row(a), PADY + u * (by - 8), 8, None, u)
+            for x0, rows in spans:
+                border(turn, x0, PADY + u * (by - 8), rows, None, u)
         each(2, along_y)
 
     for copy in local(0):
@@ -431,6 +432,7 @@
     def first_row(a):
         for copy in local(a + 1):
             copy.wait()
+        pl.when(a == n_a // 2)(greet)
 
         def block(x0, q, following):
             y0 = column(q)
@@ -441,42 +443,52 @@
             return coefficients(x0, y0, 8, emit, following)
         chain(block, range(1, n_q - 1), row(a))
     each(n_a, first_row)
-    middle = range(2, n_a - 2)
-    ends = [a for a in range(n_a) if a not in middle]
-
-    def correct(turn, frame, along_y, along_x):
-        second_inner()
-        wait_recv(along_y)
+    edge = 14
+    part = (bx - 2 * edge) // 4
+
+    def restart(x0, rows, q, following):
+        y0 = column(q)
+
+        def emit(i, total, centre):
+            x = x0 + i
+            put(b, x, y0, at(w, x, y0) * (at(r, x, y0) + total) - centre)
+        return stencil(pr, x0, y0, rows, emit, following)
+
+    def correct_middle(turn, frame):
         frame_y(frame)
         second_ends()
         strips_along_y(*range(1, bx // 8 - 1))
-        border_y(turn, *middle)
-        each(n_a - 2, third_inner(turn), 2)
-        wait_recv(along_x)
+        border_y(turn, *[(PADX + edge + part * n, part) for n in range(4)])
+        each(4, lambda n: third_rows(turn, PADX + edge + part * n, part))
+
+    def correct_border(turn, frame):
         frame_x(frame)
         second_rows()
         strips_along_x()
         strips_along_y(0, bx // 8 - 1)
         border_x(turn)
-        border_y(turn, *ends)
+        border_y(turn, (PADX + 4, edge - 4), (PADX + bx - edge, edge - 4))
 
     def third_ends(turn):
-        each(4, lambda n: third_inner(turn)(n + (n // 2) * (n_a - 4)))
-
-    correct(0, frame_first, halos_y, halos_x)
+        each(2, lambda t: third_rows(turn, PADX + 4 + t * (bx - 4 - edge), edge - 4))
+
+    each(n_a - 1, second_row, 1)
+    wait_recv(halos_y)
+    correct_middle(0, frame_first)
+    early = 16
+    each((bx - 2 * early) // 8, lambda n: chain(restart, range(1, n_q - 1), PADX + early + 8 * n, 8))
+    each(n_a - 2, second_row, 2)
+    wait_recv(halos_x)
+    correct_border(0, frame_first)
     spread = [halo(pr, PADX, PADY, pr, d, 3) for d in (*DIRS[2:4], *DIRS[0:2], *DIRS[4:])]
     start(spread)
     third_ends(0)
-
-    def restart(x0, q, following):
-        y0 = column(q)
-
-        def emit(i, total, centre):
-            x = x0 + i
-            put(b, x, y0, at(w, x, y0) * (at(r, x, y0) + total) - centre)
-        return stencil(pr, x0, y0, 8, emit, following)
-    each(n_a, lambda a: chain(restart, range(1, n_q - 1), row(a)))
-    correct(1, frame_again, spread[:2], spread[2:])
+    each(2, lambda t: chain(restart, range(1, n_q - 1), PADX + 4 + t * (bx - 4 - early), early - 4))
+    each(2, lambda t: second_row(1 + t * (n_a - 3)))
+    wait_recv(spread[:2])
+    correct_middle(1, frame_again)
+    wait_recv(spread[2:])
+    correct_border(1, frame_again)
     third_ends(1)
     wait_send(halos_y)
     wait_send(halos_x)

time: 39.7 us -> 43.5 us (1.096)
  the two profiles are of different devices: /device:TPU:19 before, /device:TPU:0 now
where the time goes in v4:
time: 43.5 us; the launch traced here: 43.3 us
  Pallas kernels  43.3 us (100%)
    pallas_call x1, Pallas kernels, shards(): pl.pallas_call(functools.partial(kernel, n_sub, n_col, bx, by), out_shape...  41.2 us
    pallas_call x1, Pallas kernels, shards(): pl.pallas_call(store, out_shape=jax.ShapeDtypeStruct((bx, by, nz), jnp.fl...  2.07 us

profile of v4, /device:TPU:0, one launch (start us, length us, event | category | flops | bytes accessed | tf_op | source)
XLA Modules:
  0.0 43.3 jit_solution(4559223371271731193)
XLA Ops:
  0.0 41.2 %shard_map.55.source = f32[64,128,128]{2,1,0:T(8,128)S(1)} custom-call(f32[64,128,128]{2,1,0:T(8,128)} %perm.1, f32[64,128,128]{2,1,0:T(8,128)} %accum.1, f32[64,128,128]{2,1,0:T(8,128)} %rhs.1, s32[2,128]{1,0:T(2,128)} %depth_x.1, s32[2,64]{1,0:T(2,128)} %bitcast.1), custom_call_target="tpu_custom_call" | custom-call | flops 125829120 | bytes 16777216 | tf_op jit(solution)/shard_map/pallas_call | solution.py:517
  41.2 2.1 %shard_map.56 = f32[64,128,128]{2,1,0:T(8,128)} custom-call(f32[64,128,128]{2,1,0:T(8,128)S(1)} %shard_map.55.source), custom_call_target="tpu_custom_call" | custom-call | tf_op jit(solution)/shard_map/pallas_call | solution.py:540

commit v5 on v3

--- a/solution.py
+++ b/solution.py
@@ -247,14 +247,14 @@
             found.append((yw.at[u], yb.at[u], x0, y0 - strip_y(u)))
         return found
 
-    def frame_first(x0, y0, rows, t, u):
+    def frame_first(x0, y0, rows, t, u, ring=False):
         j = y0 - PADY + sublane
         in_y = (j >= 0) & (j < by)
         if t is not None:
             deep_x = dx_ref[t, pl.ds(y0, 8), :]
         if u is not None:
             m_y = jnp.where(u == 0, j, by - 1 - j)
-        if t is not None and u is not None:
+        if ring and t is not None and u is not None:
             corner_x = (m_y == -1) & (end_y(t, u) >= 1)
             corner_y = (m_y == -1) & (end_x(u, t) >= 1)
 
@@ -269,7 +269,7 @@
                 beyond = m < 0
                 member = jnp.where(beyond, -1 - m, jnp.where(in_y, -1, 8)) < deep_x
                 other = jnp.where(beyond, jnp.where(in_y, -1, 8), m) < deep_x
-                if u is not None:
+                if ring and u is not None:
                     other = other | (corner_x & (m == -1))
                 weight = jnp.where(other, inverse, 0.0)
                 put(xw.at[t], x - strip_x(t), y0, weight)
@@ -279,7 +279,7 @@
                 inside = jnp.where((i >= 0) & (i < bx), 0, 8)
                 member = member | (jnp.where(m_y < 0, -1 - m_y, 8) < deep_y)
                 other = jnp.where(m_y < 0, inside - 1, m_y) < deep_y
-                if t is not None:
+                if ring and t is not None:
                     other = other | (corner_y & (m == -1))
                 weight = jnp.where(other, inverse, 0.0)
                 put(yw.at[u], x, y0 - strip_y(u), weight)
@@ -289,7 +289,7 @@
             put(b, x, y0, weight * source)
         coefficients(x0, y0, rows, emit)
 
-    def frame_again(x0, y0, rows, t, u):
+    def frame_again(x0, y0, rows, t, u, ring=False):
         def emit(n, total, centre):
             x = x0 + n
             total = at(r, x, y0) + total
@@ -304,18 +304,18 @@
     def column(q):
         return PADY - 4 + 8 * q
 
-    def frame_x(block):
-        unroll = 5 if (n_q - 2) % 5 == 0 else 1
-
-        def along_x(n):
-            t, q = n // ((n_q - 2) // unroll), n % ((n_q - 2) // unroll)
-            for v in range(unroll):
-                block(PADX - 2 + t * (bx - 2), column(1 + q * unroll + v), 6, t, None)
-        each(2 * ((n_q - 2) // unroll), along_x)
+    def frame_x(block, ring):
+        def first(t):
+            return PADX - 2 + t * (bx + 1) if ring else PADX + 1 + t * (bx - 5)
+
+        def along_x(t):
+            for q in range(1, n_q - 1):
+                block(first(t), column(q), 3, t, None, ring)
+        each(2, along_x)
 
         def corner(n):
             t, u = n // 2, n % 2
-            block(PADX - 2 + t * (bx - 2), column(u * (n_q - 1)), 6, t, u)
+            block(first(t), column(u * (n_q - 1)), 3, t, u, ring)
         each(4, corner)
 
     def frame_y(block):
@@ -345,8 +345,10 @@
             chain(second, range(0, 2), row(a + 1), 8)
         each(n_a - 2, ends)
 
+    def second_next():
+        each(2, lambda t: chain(second, range(n_q), PADX + 4 + t * (bx - 16), 8))
+
     def second_rows():
-        each(2, lambda t: chain(second, range(n_q), PADX + 4 + t * (bx - 16), 8))
         each(2, lambda t: chain(second, range(n_q), PADX - 1 + t * (bx - 3), 5))
 
     def strip(src, dst, weight, x0, y0, rows, following, lx, ly):
@@ -448,12 +450,14 @@
         second_inner()
         wait_recv(along_y)
         frame_y(frame)
+        frame_x(frame, False)
         second_ends()
+        second_next()
         strips_along_y(*range(1, bx // 8 - 1))
         border_y(turn, *middle)
         each(n_a - 2, third_inner(turn), 2)
         wait_recv(along_x)
-        frame_x(frame)
+        frame_x(frame, True)
         second_rows()
         strips_along_x()
         strips_along_y(0, bx // 8 - 1)

time: 39.7 us -> 38.8 us (0.977); the launches traced: 39.5 us -> 38.1 us
  Pallas kernels: 39.5 us -> 38.1 us
    pallas_call x1, Pallas kernels: 37.5 us -> 36 us  [shards(): pl.pallas_call(functools.partial(kernel, n_sub, n_col, bx, by), out_shape...]
where the time goes in v5:
time: 38.8 us; the launch traced here: 38.1 us
  Pallas kernels  38.1 us (98%)
    pallas_call x1, Pallas kernels, shards(): pl.pallas_call(functools.partial(kernel, n_sub, n_col, bx, by), out_shape...  36 us
    pallas_call x1, Pallas kernels, shards(): pl.pallas_call(store, out_shape=jax.ShapeDtypeStruct((bx, by, nz), jnp.fl...  2.07 us

profile of v5, /device:TPU:19, one launch (start us, length us, event | category | flops | bytes accessed | tf_op | source)
XLA Modules:
  0.0 38.1 jit_solution(4740406983032852142)
XLA Ops:
  0.0 36.0 %shard_map.55.source = f32[64,128,128]{2,1,0:T(8,128)S(1)} custom-call(f32[64,128,128]{2,1,0:T(8,128)} %perm.1, f32[64,128,128]{2,1,0:T(8,128)} %accum.1, f32[64,128,128]{2,1,0:T(8,128)} %rhs.1, s32[2,128]{1,0:T(2,128)} %depth_x.1, s32[2,64]{1,0:T(2,128)} %bitcast.1), custom_call_target="tpu_custom_call" | custom-call | flops 125829120 | bytes 16777216 | tf_op jit(solution)/shard_map/pallas_call | solution.py:509
  36.0 2.1 %shard_map.56 = f32[64,128,128]{2,1,0:T(8,128)} custom-call(f32[64,128,128]{2,1,0:T(8,128)S(1)} %shard_map.55.source), custom_call_target="tpu_custom_call" | custom-call | tf_op jit(solution)/shard_map/pallas_call | solution.py:532

commit v6 on v5

--- a/solution.py
+++ b/solution.py
@@ -485,16 +485,6 @@
     wait_send(halos_y)
     wait_send(halos_x)
     wait_send(spread)
-
-
-def store(source, target, sem):
-    rows = source.shape[0] // 8
-    copies = [pltpu.make_async_copy(source.at[pl.ds(i * rows, rows)], target.at[pl.ds(i * rows, rows)], sem.at[i])
-              for i in range(8)]
-    for copy in copies:
-        copy.start()
-    for copy in copies:
-        copy.wait()
 
 
 def shards(n_sub, n_col, perm, accum, rhs, depth_x, depth_y):
@@ -529,13 +519,7 @@
         cost_estimate=pl.CostEstimate(
             flops=120 * bx * by * nz, bytes_accessed=16 * bx * by * nz, transcendentals=0),
     )(perm, accum, rhs, depth_x, depth_y.T)
-    return pl.pallas_call(
-        store,
-        out_shape=jax.ShapeDtypeStruct((bx, by, nz), jnp.float32),
-        in_specs=[vmem], out_specs=hbm,
-        scratch_shapes=[pltpu.SemaphoreType.DMA((8,))],
-        compiler_params=pltpu.CompilerParams(vmem_limit_bytes=4 * 1024 * 1024),
-    )(result)
+    return result
 
 
 def solution(mesh):

time: 38.8 us -> 38.7 us (level)
  Pallas kernels: 38.1 us -> 36 us
  local copies, waits for them, and re-layouts: 0 us -> 2.02 us
    pallas_call x1 -> x0, Pallas kernels: 2.07 us -> none  [shards(): pl.pallas_call(store, out_shape=jax.ShapeDtypeStruct((bx, by, nz), jnp.fl...]
    unnamed x0 -> x1, local copies, waits for them, and re-layouts: none -> 2.02 us
where the time goes in v6:
time: 38.7 us; the launch traced here: 38.1 us
  Pallas kernels  36 us (93%)
  local copies, waits for them, and re-layouts  2.02 us (5%)
    pallas_call x1, Pallas kernels, shards(): pl.pallas_call(functools.partial(kernel, n_sub, n_col, bx, by), out_shape...  36 us
    unnamed x1, local copies, waits for them, and re-layouts  2.02 us

profile of v6, /device:TPU:19, one launch (start us, length us, event | category | flops | bytes accessed | tf_op | source)
XLA Modules:
  0.0 38.1 jit_solution(16049418279507225643)
XLA Ops:
  0.0 36.0 %shard_map.55 = f32[64,128,128]{2,1,0:T(8,128)S(1)} custom-call(f32[64,128,128]{2,1,0:T(8,128)} %perm.1, f32[64,128,128]{2,1,0:T(8,128)} %accum.1, f32[64,128,128]{2,1,0:T(8,128)} %rhs.1, s32[2,128]{1,0:T(2,128)} %depth_x.1, s32[2,64]{1,0:T(2,128)} %bitcast.1), custom_call_target="tpu_custom_call" | custom-call | flops 125829120 | bytes 16777216 | tf_op jit(solution)/shard_map/pallas_call | solution.py:499
  36.0 2.0 %copy.7 = f32[64,128,128]{2,1,0:T(8,128)} copy(f32[64,128,128]{2,1,0:T(8,128)S(1)} %shard_map.55) | data formatting | bytes 8388608
